TPU v7x, 512 devices: a whole 4x4x16 slice. The times are simulated.
512 devices in a mesh: dp: 16 (over z), head: 8 (over x, core), srv: 4 (over y).
Axes of the slice: x: 4, y: 4, z: 16, core: 2. Of those that a mesh axis runs over, the one named last changes fastest.
Arguments:
- queries: bfloat16 [2048, 8, 1024], P('dp', 'srv', 'head'), may hold values from -5 to 5
- keys: bfloat16 [10240, 1024], P(('dp', 'head')), may hold values from -5 to 5
- values: bfloat16 [10240, 1024], P(('dp', 'head')), may hold values from -6 to 6
- output_gradient: bfloat16 [2048, 8, 1024], P('dp', 'srv', 'head'), may hold values from -6 to 6
- doc_ids: int32 [10240], P('dp'), may hold values from 0 to 7, never falling along the last dimension, each value on 1 to 5120 neighbouring positions
Outputs:
- attention: bfloat16 [2048, 8, 1024], P('dp', 'srv', 'head')
- q_grad: bfloat16 [2048, 8, 1024], P('dp', 'srv', 'head')
- k_grad: bfloat16 [10240, 1024], P(('dp', 'head', 'srv'))
- v_grad: bfloat16 [10240, 1024], P(('dp', 'head', 'srv'))
Inputs may be any that keep to these rules, and one draw needn't show every extreme that they name: `doc_ids`: document numbers never fall along the keys; every document holds at most 5120 keys, and one holds exactly 5120.
All inputs are finite; a program needn't handle non-finite values.
Results may differ from a plain program's by a relative error of at most 0.039.
Values may be sent and summed in bfloat16 or wider, within the bound.
No kernel may reach another device: no remote copies, remote signals or barrier semaphores. Data moves between devices by JAX's collectives and lax.ppermute only.
A program may use at most 64 MiB of HBM per device.

v0:
```python
import math
import jax
import jax.numpy as jnp
from jax import lax
from jax.sharding import PartitionSpec as P

HEAD_SIZE = 128
NEGATIVE = -1e30


def local(queries, keys, values, output_gradient, doc_ids):
    home_rows, pair_heads, group_width = queries.shape
    groups = group_width // HEAD_SIZE
    scale_factor = HEAD_SIZE ** (-0.5)
    key_rows, value_rows = (
        lax.all_to_all(keys, "head", split_axis=1, concat_axis=0, tiled=True),
        lax.all_to_all(values, "head", split_axis=1, concat_axis=0, tiled=True),
    )
    key_count = key_rows.shape[0]
    servers = lax.axis_size("dp")
    server = lax.axis_index("dp")
    key_at = server * key_count + jnp.arange(key_count, dtype=jnp.int32)
    all_docs = lax.all_gather(doc_ids, "dp", axis=0, tiled=True)
    query_total = home_rows * servers
    context = all_docs.shape[0] - query_total
    query_docs = all_docs[context:]
    query_places = context + jnp.arange(query_total, dtype=jnp.int32)
    all_q, all_dout = (
        lax.all_gather(queries, "dp", axis=0, tiled=True),
        lax.all_gather(output_gradient, "dp", axis=0, tiled=True),
    )
    block_rows = math.gcd(512, query_total)
    block_count = query_total // block_rows
    key_heads = key_rows.reshape(key_count, groups, HEAD_SIZE)
    value_heads = value_rows.reshape(key_count, groups, HEAD_SIZE)
    query_blocks = all_q.reshape(block_count, block_rows, pair_heads, groups, HEAD_SIZE)
    grad_blocks = all_dout.reshape(block_count, block_rows, pair_heads, groups, HEAD_SIZE)
    place_blocks = query_places.reshape(block_count, block_rows)
    doc_blocks = query_docs.reshape(block_count, block_rows)

    def admissible(places, query_doc):
        return (key_at[None, :] <= places[:, None]) & (doc_ids[None, :] == query_doc[:, None])

    def scores_of(query_block):
        return (
            jnp.einsum("pjgd,kgd->gjpk", query_block, key_heads, preferred_element_type=jnp.float32)
            * scale_factor
        )

    def block_max(inputs):
        query_block, places, query_doc = inputs
        allowed = admissible(places, query_doc)

        def compute():
            raw_scores = scores_of(query_block)
            masked = jnp.where(allowed[None, None], raw_scores, NEGATIVE)
            return (jnp.max(masked, axis=-1).transpose(2, 1, 0), raw_scores)

        return compute()

    def block_top(inputs):
        return block_max(inputs)[0]

    local_max = lax.map(block_top, (query_blocks, place_blocks, doc_blocks))
    row_max = lax.pmax(local_max.reshape(query_total, pair_heads, groups), "dp")
    max_blocks = row_max.reshape(block_count, block_rows, pair_heads, groups)

    def block_sum(inputs):
        stored, places, query_doc, row_top = inputs
        allowed = admissible(places, query_doc)

        def compute():
            block_scores = scores_of(stored)
            shifted = block_scores - row_top.transpose(2, 1, 0)[..., None]
            weights = jnp.where(allowed[None, None], jnp.exp(shifted), 0.0)
            weighted = jnp.einsum(
                "gjpk,kgd->pjgd",
                weights.astype(jnp.bfloat16),
                value_heads,
                preferred_element_type=jnp.float32,
            )
            return (
                weighted.reshape(block_rows, pair_heads, group_width),
                jnp.sum(weights, axis=-1).transpose(2, 1, 0),
            )

        return compute()

    part_out, part_norm = lax.map(block_sum, (query_blocks, place_blocks, doc_blocks, max_blocks))
    part_out = part_out.reshape(query_total, pair_heads, group_width)
    part_norm = part_norm.reshape(query_total, pair_heads, groups)
    home_out, home_norm = (
        lax.psum_scatter(part_out, "dp", scatter_dimension=0, tiled=True),
        lax.psum_scatter(part_norm, "dp", scatter_dimension=0, tiled=True),
    )
    home_max = lax.dynamic_slice_in_dim(row_max, server * home_rows, home_rows, 0)
    attn_home = (
        home_out.reshape(home_rows, pair_heads, groups, HEAD_SIZE) / home_norm[..., None]
    ).astype(jnp.bfloat16)
    log_home = home_max + jnp.log(home_norm)
    grad_home = output_gradient.reshape(home_rows, pair_heads, groups, HEAD_SIZE).astype(
        jnp.float32
    )
    delta_home = jnp.sum(grad_home * attn_home.astype(jnp.float32), axis=-1)
    log_all, delta_all = (
        lax.all_gather(log_home, "dp", axis=0, tiled=True),
        lax.all_gather(delta_home, "dp", axis=0, tiled=True),
    )
    attention = attn_home.reshape(home_rows, pair_heads, group_width)
    log_blocks = log_all.reshape(block_count, block_rows, pair_heads, groups)
    delta_blocks = delta_all.reshape(block_count, block_rows, pair_heads, groups)

    def block_grad(totals, inputs):
        query_block, grad_block, places, query_doc, log_norm, row_delta = inputs
        allowed = admissible(places, query_doc)

        def compute():
            shifted = scores_of(query_block) - log_norm.transpose(2, 1, 0)[..., None]
            probs = jnp.where(allowed[None, None], jnp.exp(shifted), 0.0)
            value_grad = jnp.einsum(
                "gjpk,pjgd->kgd",
                probs.astype(jnp.bfloat16),
                grad_block,
                preferred_element_type=jnp.float32,
            )
            weight_grad = jnp.einsum(
                "pjgd,kgd->gjpk", grad_block, value_heads, preferred_element_type=jnp.float32
            )
            score_grad = (probs * (weight_grad - row_delta.transpose(2, 1, 0)[..., None])).astype(
                jnp.bfloat16
            )
            query_grad = (
                jnp.einsum(
                    "gjpk,kgd->pjgd", score_grad, key_heads, preferred_element_type=jnp.float32
                )
                * scale_factor
            )
            key_grad = (
                jnp.einsum(
                    "gjpk,pjgd->kgd", score_grad, query_block, preferred_element_type=jnp.float32
                )
                * scale_factor
            )
            return (query_grad.reshape(block_rows, pair_heads, group_width), key_grad, value_grad)

        query_grad, key_grad, value_grad = compute()
        return ((totals[0] + key_grad, totals[1] + value_grad), query_grad)

    zero_start = jnp.zeros((key_count, groups, HEAD_SIZE), jnp.float32)
    grad_inputs = (query_blocks, grad_blocks, place_blocks, doc_blocks, log_blocks, delta_blocks)
    (key_total, value_total), query_parts = lax.scan(
        block_grad, (zero_start, zero_start), grad_inputs
    )
    q_summed = lax.psum_scatter(
        query_parts.reshape(query_total, pair_heads, group_width).astype(jnp.bfloat16),
        "dp",
        scatter_dimension=0,
        tiled=True,
    )
    spread_key, spread_value = (
        lax.all_to_all(
            key_total.reshape(key_count, group_width).astype(jnp.bfloat16),
            "head",
            split_axis=0,
            concat_axis=1,
            tiled=True,
        ).astype(jnp.float32),
        lax.all_to_all(
            value_total.reshape(key_count, group_width).astype(jnp.bfloat16),
            "head",
            split_axis=0,
            concat_axis=1,
            tiled=True,
        ).astype(jnp.float32),
    )
    k_summed, v_summed = (
        lax.psum_scatter(
            spread_key.astype(jnp.bfloat16), "srv", scatter_dimension=0, tiled=True
        ).astype(jnp.float32),
        lax.psum_scatter(
            spread_value.astype(jnp.bfloat16), "srv", scatter_dimension=0, tiled=True
        ).astype(jnp.float32),
    )
    return (attention, q_summed, k_summed.astype(jnp.bfloat16), v_summed.astype(jnp.bfloat16))


def solution(mesh):
    placed = (
        P("dp", "srv", "head"),
        P(("dp", "head"), None),
        P(("dp", "head"), None),
        P("dp", "srv", "head"),
        P("dp"),
    )
    return jax.shard_map(
        local,
        mesh=mesh,
        in_specs=placed,
        out_specs=(
            P("dp", "srv", "head"),
            P("dp", "srv", "head"),
            P(("dp", "head", "srv"), None),
            P(("dp", "head", "srv"), None),
        ),
        check_vma=False,
    )
```

profile of v0, /device:TPU:2, one launch (start us, length us, event | category | flops | bytes accessed | tf_op | source)
XLA Modules:
  0.0 651.0 jit_solution(6897663471784736279)
XLA Ops:
  7.2 1.5 copy.61
  9.5 9.2 %all-to-all-start = ((bf16[80,8,128]{2,0,1:T(8,128)(2,1)}), bf16[80,8,128]{2,0,1:T(8,128)(2,1)S(1)}, u32[]{:S(2)}, u32[]{:S(2)}) async-start(bf16[80,8,128]{2,0,1:T(8,128)(2,1)} %copy_bitcast_fusion.3), calls=%async_computation | async-start | bytes 327680 | tf_op jit(solution)/shard_map/all_to_all | solution.py:16
  18.7 1.6 copy_bitcast_fusion.2
  21.0 31.2 %all-gather.1 = s32[16,1,640]{2,1,0:T(1,128)S(1)} all-gather(s32[1,1,640]{2,1,0:T(1,128)S(1)} %reshape.364), channel_id=1, replica_groups=mesh['dp'=16,'head'=8,'srv'=4] {'dp'}, dimensions={0}, use_global_device_ids=true | all-gather | bytes 43520 | tf_op jit(solution)/shard_map/all_gather | solution.py:23
  52.8 33.4 %all-gather.5.cloned.1.call-done = bf16[2048,2,128]{2,0,1:T(8,128)(2,1)} async-done(((bf16[128,2,128]{2,0,1:T(8,128)(2,1)}), bf16[2048,2,128]{2,0,1:T(8,128)(2,1)}) %all-gather.5.cloned.1.call-update) | async-done | bytes 1048592 | tf_op jit(solution)/shard_map/all_gather | solution.py:29
  86.3 1.3 copy.66
  87.6 4.8 all-to-all-start.1
  92.4 7.6 %while.39 = (s32[]{:T(128)}, f32[4,512,2,1]{1,0,2,3:T(4,128)S(1)}, s32[4,512]{1,0:T(4,128)}, s32[640]{0:T(1024)S(1)}, s32[4,512]{1,0:T(4,128)S(1)}, /*index=5*/b...) while((s32[]{:T(128)}, f32[4,512,2,1]{1,0,2,3:T(4,128)S(1)}, ...), condition=%wide.region_2.3_spmd.clone, body=%wide.region_0.2_spmd.clone.sunk | while | flops 170720896 | bytes 1121917 | solution.py:64
  92.4 0.7 constant_dynamic-slice_fusion.12
  93.5 0.8 fusion.104
  94.3 0.7 constant_dynamic-slice_fusion.12
  95.4 0.8 fusion.104
  96.2 0.7 constant_dynamic-slice_fusion.12
  97.3 0.8 fusion.104
  99.2 0.8 fusion.104
  100.0 55.1 %pmax.7 = f32[2048,2,1]{0,1,2:T(2,128)} all-reduce(f32[2048,2,1]{0,1,2:T(2,128)S(1)} %reshape.354), channel_id=1, replica_groups=mesh['dp'=16,'head'=8,'srv'=4] {'dp'}, use_global_device_ids=true, to_apply=%region_3.4 | all-reduce | flops 4096 | bytes 32768 | tf_op jit(solution)/shard_map/pmax | solution.py:65
  155.1 22.3 %while.40 = (s32[]{:T(128)}, f32[4,512,2,128]{3,2,1,0:T(2,128)S(1)}, f32[4,512,2,1]{1,3,2,0:T(1,128)}, s32[4,512]{1,0:T(4,128)}, s32[640]{0:T(1024)S(1)}, /*inde...) while((s32[]{:T(128)}, ...), condition=%wide.region_6.7_spmd.clone, body=%wide.region_4.6_spmd.clone.sunk | while | flops 341769856 | bytes 8437397 | solution.py:89
  156.9 1.1 fusion.107
  157.9 1.7 fusion.108
  162.4 1.0 fusion.107
  163.5 1.7 fusion.108
  168.0 1.0 fusion.107
  169.1 1.7 fusion.108
  173.6 1.0 fusion.107
  174.6 1.7 fusion.108
  177.4 2.1 copy.88
  181.1 1.3 dynamic-slice
  183.0 63.6 %reduce-scatter.8.cloned.1.call-done = f32[128,2]{1,0:T(8,128)} async-done(((f32[2048,2]{1,0:T(8,128)}), f32[128,2]{1,0:T(8,128)}) %reduce-scatter.8.cloned.1.call-update) | async-done | bytes 1040
  246.6 0.9 copy.87
  248.3 27.4 %all_gather.17 = f32[2048,2,1]{0,1,2:T(2,128)S(1)} all-gather(f32[128,2,1]{0,1,2:T(2,128)S(1)} %log_add_fusion), channel_id=1, replica_groups=mesh['dp'=16,'head'=8,'srv'=4] {'dp'}, dimensions={0}, use_global_device_ids=true | all-gather | bytes 17408 | tf_op jit(solution)/shard_map/all_gather | solution.py:106
  275.7 115.2 %all-reduce.10.cloned.1.call-done = f32[2048,2,128]{2,1,0:T(2,128)} async-done(((f32[2048,2,128]{2,1,0:T(2,128)}), f32[2048,2,128]{2,1,0:T(2,128)}) %all-reduce.10.cloned.1.call-update) | async-done | bytes 2097168
  390.9 1.7 multiply_reduce_fusion
  392.6 35.8 %all-gather = f32[2048,2]{1,0:T(8,128)S(1)} all-gather(f32[128,2]{1,0:T(8,128)S(1)} %get-tuple-element.445), channel_id=2, replica_groups=mesh['dp'=16,'head'=8,'srv'=4] {'dp'}, dimensions={0}, use_global_device_ids=true | all-gather | bytes 17408 | tf_op jit(solution)/shard_map/all_gather | solution.py:107
  428.7 32.1 %all-gather.7.cloned.1.call-done = bf16[2048,2,128]{2,0,1:T(8,128)(2,1)} async-done(((bf16[128,2,128]{2,0,1:T(8,128)(2,1)}), bf16[2048,2,128]{2,0,1:T(8,128)(2,1)}) %all-gather.7.cloned.1.call-update) | async-done | bytes 1048592 | tf_op jit(solution)/shard_map/all_gather | solution.py:30
  460.8 37.4 %while.41 = (s32[]{:T(128)}, f32[640,1,128]{0,2,1:T(8,128)S(1)}, f32[640,1,128]{0,2,1:T(8,128)}, bf16[4,512,2,128]{3,1,2,0:T(8,128)(2,1)}, bf16[4,512,2,1,128]{4...) while((s32[]{:T(128)}, f32[640,1,128]{0,2,1:T(8,128)S(1)}, ...), condition=%wide.region_11.12_spmd.clone, body=%wide.region_10.11_spmd.clone.sunk | while | flops 846938752 | bytes 35077916 | solution.py:151
  461.4 0.8 constant_dynamic-slice_fusion.14
  462.5 2.0 fusion.120
  465.0 3.6 fusion.122
  469.2 1.0 copy-done.5
  470.7 0.8 constant_dynamic-slice_fusion.14
  471.8 2.0 fusion.120
  474.4 3.6 fusion.122
  478.5 1.0 copy-done.5
  480.1 0.8 constant_dynamic-slice_fusion.14
  481.1 2.0 fusion.120
  483.7 3.6 fusion.122
  487.9 1.0 copy-done.5
  489.4 0.8 constant_dynamic-slice_fusion.14
  490.5 2.0 fusion.120
  493.1 3.6 fusion.122
  497.2 1.0 copy-done.5
  498.2 0.8 copy.78
  499.0 4.9 all-to-all-start.2
  503.9 3.3 copy.77
  507.2 0.8 copy.80
  508.0 0.9 all-to-all-done.2
  508.9 4.8 all-to-all-start.3
  513.7 5.0 all-to-all-done.3
  518.8 12.6 %fusion.72 = (bf16[24,1024]{1,0:T(8,128)(2,1)S(1)}, bf16[24,1024]{1,0:T(8,128)(2,1)S(1)}) fusion(bf16[80,1024]{1,0:T(8,128)(2,1)S(1)} %copy_bitcast_fusion.1, bf16[80,1024]{1,0:T(8,128)(2,1)S(1)} %copy_bitcast_fusion), kind=kCustom, calls=%all-reduce-scatter.2 | all-reduce-scatter fusion | flops 196609 | bytes 428032
  531.4 1.6 collective-permute-start
  533.0 3.1 collective-permute-start.1
  536.0 1.3 dynamic-slice.10
  539.6 103.4 %all-reduce.12.cloned.1.call-done = bf16[2048,2,128]{2,1,0:T(2,128)(2,1)} async-done(((bf16[2048,2,128]{2,1,0:T(2,128)(2,1)}), bf16[2048,2,128]{2,1,0:T(2,128)(2,1)}) %all-reduce.12.cloned.1.call-update) | async-done | bytes 1048592
  643.0 1.5 constant_dynamic-slice_fusion.8
  (133 shorter events, 27.3 us)
Async XLA Ops:
  7.2 1.6 copy-start
  7.2 85.2 %copy-start.3 = (s32[640]{0:T(1024)S(1)}, s32[640]{0:T(1024)}, u32[]{:S(2)}) copy-start(s32[640]{0:T(1024)} %param.15) | copy-start | bytes 7684
  7.2 79.1 %all-gather.5.cloned.1.call-start = ((), (), s32[]{:S(2)}) async-start(), calls=%async_computation.5 | async-start | bytes 1114112 | tf_op jit(solution)/shard_map/all_gather | solution.py:29
  9.5 78.1 %all-to-all-start = ((bf16[80,8,128]{2,0,1:T(8,128)(2,1)}), bf16[80,8,128]{2,0,1:T(8,128)(2,1)S(1)}, u32[]{:S(2)}, u32[]{:S(2)}) async-start(bf16[80,8,128]{2,0,1:T(8,128)(2,1)} %copy_bitcast_fusion.3), calls=%async_computation | async-start | bytes 327680 | tf_op jit(solution)/shard_map/all_to_all | solution.py:16
  87.6 67.6 %all-to-all-start.1 = ((bf16[80,8,128]{2,0,1:T(8,128)(2,1)}), bf16[80,8,128]{2,0,1:T(8,128)(2,1)}, u32[]{:S(2)}, u32[]{:S(2)}) async-start(bf16[80,8,128]{2,0,1:T(8,128)(2,1)} %copy_bitcast_fusion.2), calls=%async_computation.1 | async-start | bytes 327680 | tf_op jit(solution)/shard_map/all_to_all | solution.py:17
  92.4 154.2 %reduce-scatter.8.cloned.1.call-start = ((), (), s32[]{:S(2)}) async-start(), calls=%async_computation.7 | async-start | bytes 1114112
  177.4 2.2 copy-start.2
  177.4 2.9 copy-start.7
  179.6 211.3 %all-reduce.10.cloned.1.call-start = ((), (), s32[]{:S(2)}) async-start(), calls=%async_computation.8 | async-start | bytes 4194304
  180.3 280.5 %all-gather.7.cloned.1.call-start = ((), (), s32[]{:S(2)}) async-start(), calls=%async_computation.6 | async-start | bytes 1114112 | tf_op jit(solution)/shard_map/all_gather | solution.py:30
  461.3 3.2 copy-start.1
  465.0 3.6 copy-start.4
  469.2 1.0 copy-start.5
  470.7 3.2 copy-start.1
  474.4 3.6 copy-start.4
  478.5 1.0 copy-start.5
  480.0 3.2 copy-start.1
  483.7 3.6 copy-start.4
  487.9 1.0 copy-start.5
  489.4 3.2 copy-start.1
  493.1 3.6 copy-start.4
  497.2 1.0 copy-start.5
  498.2 9.0 %copy-start.6 = (f32[640,1,128]{0,2,1:T(8,128)S(1)}, f32[640,1,128]{0,2,1:T(8,128)}, u32[]{:S(2)}) copy-start(f32[640,1,128]{0,2,1:T(8,128)} %get-tuple-element.183) | copy-start | bytes 983044
  499.0 9.9 %all-to-all-start.2 = ((bf16[8,80,128]{2,1,0:T(8,128)(2,1)}), bf16[8,80,128]{2,1,0:T(8,128)(2,1)S(1)}, u32[]{:S(2)}, u32[]{:S(2)}) async-start(bf16[8,80,128]{2,1,0:T(8,128)(2,1)} %bitcast.15), calls=%async_computation.2 | async-start | bytes 327680 | tf_op jit(solution)/shard_map/all_to_all | solution.py:161
  503.9 139.1 %all-reduce.12.cloned.1.call-start = ((), (), s32[]{:S(2)}) async-start(), calls=%async_computation.9 | async-start | bytes 2097152
  508.9 9.8 %all-to-all-start.3 = ((bf16[8,80,128]{2,1,0:T(8,128)(2,1)}), bf16[8,80,128]{2,1,0:T(8,128)(2,1)S(1)}, u32[]{:S(2)}, u32[]{:S(2)}) async-start(bf16[8,80,128]{2,1,0:T(8,128)(2,1)} %bitcast.17), calls=%async_computation.3 | async-start | bytes 327680 | tf_op jit(solution)/shard_map/all_to_all | solution.py:168
  531.4 6.6 %collective-permute-start = (bf16[12,1024]{1,0:T(8,128)(2,1)S(1)}, bf16[12,1024]{1,0:T(8,128)(2,1)S(1)}, u32[]{:S(2)}, u32[]{:S(2)}) collective-permute-start(bf16[12,1024]{1,0:T(8,128)(2,1)S(1)} %slice.16), channel_id=1, source_target_pairs={{0,1},{1,2},{2,3},{4,5},{5,6},{6,7},{8,9},{9,10},{10,11},{12,13},{... | collective-permute-start | bytes 73736
  533.0 5.2 collective-permute-start.1
Sparse Core Ops, SparseCore 0:
  10.7 75.5 all-gather.4
  179.7 66.8 reduce-scatter.7
  249.1 141.7 all-reduce.9
  393.6 67.1 all-gather.6
  507.3 135.5 all-reduce.11
where the time goes:
time: 653 us; the launch traced here: 651 us
  waiting for transfers between devices  354 us (54%)
  blocking collectives  162 us (25%)
  matrix products  42.8 us (7%)
  local copies, waits for them, and re-layouts  40.5 us (6%)
  starting transfers between devices  28.4 us (4%)
  between operations  15.3 us (2%)
  other arithmetic  7 us (1%)
    unnamed x10, waiting for transfers between devices  283 us
    pmax x1, blocking collectives, local(): row_max = lax.pmax(local_max.reshape(query_total, pair_heads, groups), 'dp')  55.1 us
    all_gather x1, blocking collectives, local(): lax.all_gather(delta_home, 'dp', axis=0, tiled=True)  35.8 us
    all_gather x1, waiting for transfers between devices, local(): lax.all_gather(queries, 'dp', axis=0, tiled=True)  33.4 us
    all_gather x1, waiting for transfers between devices, local(): lax.all_gather(output_gradient, 'dp', axis=0, tiled=True)  32.1 us
    all_gather x1, blocking collectives, local(): all_docs = lax.all_gather(doc_ids, 'dp', axis=0, tiled=True)  31.2 us
    all_gather x1, blocking collectives, local(): lax.all_gather(log_home, 'dp', axis=0, tiled=True)  27.4 us
    dot_general x4, matrix products, compute(): jnp.einsum('gjpk,pjgd->kgd', probs.astype(jnp.bfloat16), grad_block, pref...  14.3 us
  transfers between devices with their start and end apart: 11, of which 7 were waited for; matrix products, arithmetic and copies ran while one was open for 6% of the time, Pallas kernels for 0%

commit v1 on v0

--- a/solution.py
+++ b/solution.py
@@ -27,7 +27,9 @@
     query_places = context + jnp.arange(query_total, dtype=jnp.int32)
     all_q, all_dout = (
         lax.all_gather(queries, "dp", axis=0, tiled=True),
-        lax.all_gather(output_gradient, "dp", axis=0, tiled=True),
+        jnp.concatenate(
+            lax.all_to_all(jnp.stack([output_gradient] * lax.axis_size("dp")), "dp", 0, 0), axis=0
+        ),
     )
     block_rows = math.gcd(512, query_total)
     block_count = query_total // block_rows

time: 653 us -> 618 us (0.946)
  waiting for transfers between devices: 354 us -> 323 us
    all_gather x1 -> x0, waiting for transfers between devices: 32.1 us -> none  [local(): lax.all_gather(output_gradient, 'dp', axis=0, tiled=True)]
    dynamic_slice x12, local copies, waits for them, and re-layouts: 8.69 us -> 0.12 us  [local(): local_max = lax.map(block_top, (query_blocks, place_blocks, doc_blocks))]
    unnamed x10 -> x9, waiting for transfers between devices: 283 us -> 284 us
    unnamed x26 -> x24, local copies, waits for them, and re-layouts: 13.2 us -> 12.7 us
  transfers between devices with their start and end apart: 11 -> 11, of which waited for: 7 -> 6; matrix products, arithmetic and copies ran while one was open for 6% -> 8% of each run, Pallas kernels for 0% -> 0%
where the time goes in v1:
time: 618 us; the launch traced here: 617 us
  waiting for transfers between devices  323 us (52%)
  blocking collectives  166 us (27%)
  matrix products  39.1 us (6%)
  local copies, waits for them, and re-layouts  34.3 us (6%)
  starting transfers between devices  32.2 us (5%)
  between operations  15.3 us (2%)
    unnamed x9, waiting for transfers between devices  284 us
    pmax x1, blocking collectives, local(): row_max = lax.pmax(local_max.reshape(query_total, pair_heads, groups), 'dp')  58 us
    all_gather x1, blocking collectives, local(): lax.all_gather(delta_home, 'dp', axis=0, tiled=True)  34.5 us
    all_gather x1, waiting for transfers between devices, local(): lax.all_gather(queries, 'dp', axis=0, tiled=True)  33.2 us
    all_gather x1, blocking collectives, local(): all_docs = lax.all_gather(doc_ids, 'dp', axis=0, tiled=True)  31.2 us
    all_gather x1, blocking collectives, local(): lax.all_gather(log_home, 'dp', axis=0, tiled=True)  29.7 us
    dot_general x4, matrix products, compute(): jnp.einsum('gjpk,pjgd->kgd', probs.astype(jnp.bfloat16), grad_block, pref...  14.2 us
    unnamed x1, blocking collectives  12.8 us
  transfers between devices with their start and end apart: 11, of which 6 were waited for; matrix products, arithmetic and copies ran while one was open for 8% of the time, Pallas kernels for 0%

profile of v1, /device:TPU:2, one launch (start us, length us, event | category | flops | bytes accessed | tf_op | source)
XLA Modules:
  0.0 616.9 jit_solution(4216063106920843114)
XLA Ops:
  7.2 1.5 copy.61
  9.5 9.2 %all-to-all-start = ((bf16[80,8,128]{2,0,1:T(8,128)(2,1)}), bf16[80,8,128]{2,0,1:T(8,128)(2,1)S(1)}, u32[]{:S(2)}, u32[]{:S(2)}) async-start(bf16[80,8,128]{2,0,1:T(8,128)(2,1)} %copy_bitcast_fusion.3), calls=%async_computation | async-start | bytes 327680 | tf_op jit(solution)/shard_map/all_to_all | solution.py:16
  18.7 1.6 copy_bitcast_fusion.2
  21.0 31.2 %all-gather.1 = s32[16,1,640]{2,1,0:T(1,128)S(1)} all-gather(s32[1,1,640]{2,1,0:T(1,128)S(1)} %reshape.362), channel_id=1, replica_groups=mesh['dp'=16,'head'=8,'srv'=4] {'dp'}, dimensions={0}, use_global_device_ids=true | all-gather | bytes 43520 | tf_op jit(solution)/shard_map/all_gather | solution.py:23
  52.2 0.8 copy.71
  53.1 33.2 %all-gather.4.cloned.1.call-done = bf16[2048,2,128]{2,0,1:T(8,128)(2,1)} async-done(((bf16[128,2,128]{2,0,1:T(8,128)(2,1)}), bf16[2048,2,128]{2,0,1:T(8,128)(2,1)}) %all-gather.4.cloned.1.call-update) | async-done | bytes 1048592 | tf_op jit(solution)/shard_map/all_gather | solution.py:29
  86.3 1.3 copy.66
  87.6 4.8 all-to-all-start.1
  92.4 4.8 while.39
  92.8 0.8 fusion.104
  94.0 0.8 fusion.104
  95.2 0.8 fusion.104
  96.4 0.8 fusion.104
  97.2 58.0 %pmax.7 = f32[2048,2,1]{0,1,2:T(2,128)S(1)} all-reduce(f32[2048,2,1]{0,1,2:T(2,128)S(1)} %reshape.353), channel_id=1, replica_groups=mesh['dp'=16,'head'=8,'srv'=4] {'dp'}, use_global_device_ids=true, to_apply=%region_3.4 | all-reduce | flops 4096 | bytes 32768 | tf_op jit(solution)/shard_map/pmax | solution.py:67
  155.2 1.2 stack.2
  156.4 3.9 all-to-all-start.2
  160.4 14.1 %while.40 = (s32[]{:T(128)}, f32[4,512,2,128]{3,2,1,0:T(2,128)}, f32[4,512,2,1]{1,3,2,0:T(1,128)S(1)}, s32[4,512]{1,0:T(4,128)S(1)}, s32[640]{0:T(1024)S(1)}, /*...) while((s32[]{:T(128)}, f32[4,512,2,128]{3,2,1,0:T(2,128)}, ...), condition=%wide.region_6.7_spmd.clone, body=%wide.region_4.6_spmd.clone.sunk | while | flops 341769856 | bytes 8437397 | solution.py:91
  160.8 1.1 fusion.107
  161.9 0.9 fusion.108
  162.8 1.2 copy_dynamic-update-slice_fusion.2
  164.3 1.1 fusion.107
  165.4 0.9 fusion.108
  166.3 1.2 copy_dynamic-update-slice_fusion.2
  167.9 1.1 fusion.107
  168.9 0.9 fusion.108
  169.8 1.2 copy_dynamic-update-slice_fusion.2
  171.4 1.1 fusion.107
  172.4 0.9 fusion.108
  173.3 1.2 copy_dynamic-update-slice_fusion.2
  174.5 1.4 copy.89
  176.7 1.3 dynamic-slice
  178.6 68.9 %reduce-scatter.8.cloned.1.call-done = f32[128,2]{1,0:T(8,128)} async-done(((f32[2048,2]{1,0:T(8,128)}), f32[128,2]{1,0:T(8,128)}) %reduce-scatter.8.cloned.1.call-update) | async-done | bytes 1040
  247.5 0.9 copy.88
  248.6 29.7 %all_gather.14 = f32[2048,2,1]{0,1,2:T(2,128)} all-gather(f32[128,2,1]{0,1,2:T(2,128)S(1)} %log_add_fusion), channel_id=1, replica_groups=mesh['dp'=16,'head'=8,'srv'=4] {'dp'}, dimensions={0}, use_global_device_ids=true | all-gather | bytes 17408 | tf_op jit(solution)/shard_map/all_gather | solution.py:108
  278.2 1.1 copy.72
  279.3 112.7 %all-reduce.10.cloned.1.call-done = f32[2048,2,128]{2,1,0:T(2,128)} async-done(((f32[2048,2,128]{2,1,0:T(2,128)}), f32[2048,2,128]{2,1,0:T(2,128)}) %all-reduce.10.cloned.1.call-update) | async-done | bytes 2097168
  392.0 1.7 multiply_reduce_fusion
  393.7 34.5 %all-gather = f32[2048,2]{1,0:T(8,128)S(1)} all-gather(f32[128,2]{1,0:T(8,128)S(1)} %get-tuple-element.445), channel_id=2, replica_groups=mesh['dp'=16,'head'=8,'srv'=4] {'dp'}, dimensions={0}, use_global_device_ids=true | all-gather | bytes 17408 | tf_op jit(solution)/shard_map/all_gather | solution.py:109
  428.6 36.8 %while.41 = (s32[]{:T(128)}, f32[640,1,128]{0,2,1:T(8,128)S(1)}, f32[640,1,128]{0,2,1:T(8,128)}, bf16[4,512,2,128]{3,1,2,0:T(8,128)(2,1)}, bf16[4,512,2,1,128]{4...) while((s32[]{:T(128)}, f32[640,1,128]{0,2,1:T(8,128)S(1)}, ...), condition=%wide.region_11.12_spmd.clone, body=%wide.region_10.11_spmd.clone.sunk | while | flops 846938752 | bytes 35077916 | solution.py:153
  430.1 2.0 fusion.120
  432.6 3.5 fusion.122
  436.8 1.0 copy-done.4
  439.3 2.0 fusion.120
  441.8 3.6 fusion.122
  446.0 1.0 copy-done.4
  448.5 2.0 fusion.120
  451.0 3.6 fusion.122
  455.1 1.0 copy-done.4
  457.7 2.0 fusion.120
  460.2 3.6 fusion.122
  464.3 1.0 copy-done.4
  465.3 0.8 copy.79
  466.1 4.6 all-to-all-start.3
  470.8 3.3 copy.78
  474.1 0.8 copy.81
  474.9 0.9 all-to-all-done.3
  475.8 4.8 all-to-all-start.4
  480.5 5.0 all-to-all-done.4
  485.6 12.8 %fusion.72 = (bf16[24,1024]{1,0:T(8,128)(2,1)S(1)}, bf16[24,1024]{1,0:T(8,128)(2,1)S(1)}) fusion(bf16[80,1024]{1,0:T(8,128)(2,1)S(1)} %copy_bitcast_fusion.1, bf16[80,1024]{1,0:T(8,128)(2,1)S(1)} %copy_bitcast_fusion), kind=kCustom, calls=%all-reduce-scatter.2 | all-reduce-scatter fusion | flops 196609 | bytes 428032
  498.5 1.3 collective-permute-start
  499.8 3.4 collective-permute-start.1
  503.2 1.3 dynamic-slice.10
  506.8 102.0 %all-reduce.12.cloned.1.call-done = bf16[2048,2,128]{2,1,0:T(2,128)(2,1)} async-done(((bf16[2048,2,128]{2,1,0:T(2,128)(2,1)}), bf16[2048,2,128]{2,1,0:T(2,128)(2,1)}) %all-reduce.12.cloned.1.call-update) | async-done | bytes 1048592
  608.8 1.5 constant_dynamic-slice_fusion.8
  (132 shorter events, 17.8 us)
Async XLA Ops:
  7.2 1.6 copy-start
  7.2 85.2 %copy-start.2 = (s32[640]{0:T(1024)S(1)}, s32[640]{0:T(1024)}, u32[]{:S(2)}) copy-start(s32[640]{0:T(1024)} %param.15) | copy-start | bytes 7684
  7.2 79.1 %all-gather.4.cloned.1.call-start = ((), (), s32[]{:S(2)}) async-start(), calls=%async_computation.6 | async-start | bytes 1114112 | tf_op jit(solution)/shard_map/all_gather | solution.py:29
  9.5 78.1 %all-to-all-start = ((bf16[80,8,128]{2,0,1:T(8,128)(2,1)}), bf16[80,8,128]{2,0,1:T(8,128)(2,1)S(1)}, u32[]{:S(2)}, u32[]{:S(2)}) async-start(bf16[80,8,128]{2,0,1:T(8,128)(2,1)} %copy_bitcast_fusion.3), calls=%async_computation | async-start | bytes 327680 | tf_op jit(solution)/shard_map/all_to_all | solution.py:16
  87.6 67.7 %all-to-all-start.1 = ((bf16[80,8,128]{2,0,1:T(8,128)(2,1)}), bf16[80,8,128]{2,0,1:T(8,128)(2,1)S(1)}, u32[]{:S(2)}, u32[]{:S(2)}) async-start(bf16[80,8,128]{2,0,1:T(8,128)(2,1)} %copy_bitcast_fusion.2), calls=%async_computation.1 | async-start | bytes 327680 | tf_op jit(solution)/shard_map/all_to_all | solution.py:17
  156.4 121.8 %all-to-all-start.2 = ((bf16[16,128,2,128]{3,1,2,0:T(8,128)(2,1)}), bf16[16,128,2,128]{3,1,2,0:T(8,128)(2,1)S(1)}, u32[]{:S(2)}, u32[]{:S(2)}) async-start(bf16[16,128,2,128]{3,1,2,0:T(8,128)(2,1)} %stack.2), calls=%async_computation.2 | async-start | bytes 2097152 | tf_op jit(solution)/shard_map/all_to_all | solution.py:31
  160.4 87.1 %reduce-scatter.8.cloned.1.call-start = ((), (), s32[]{:S(2)}) async-start(), calls=%async_computation.7 | async-start | bytes 1114112
  175.9 216.1 %copy-start.6 = (bf16[128,2,128]{2,1,0:T(2,128)(2,1)S(1)}, bf16[128,2,128]{2,1,0:T(2,128)(2,1)}, u32[]{:S(2)}) copy-start(bf16[128,2,128]{2,1,0:T(2,128)(2,1)} %param.14) | copy-start | bytes 196612
  175.9 216.1 %all-reduce.10.cloned.1.call-start = ((), (), s32[]{:S(2)}) async-start(), calls=%async_computation.8 | async-start | bytes 4194304
  429.1 3.0 copy-start.1
  432.6 3.5 copy-start.3
  436.7 1.0 copy-start.4
  438.3 3.0 copy-start.1
  441.8 3.6 copy-start.3
  445.9 1.0 copy-start.4
  447.5 3.0 copy-start.1
  451.0 3.6 copy-start.3
  455.1 1.0 copy-start.4
  456.6 3.0 copy-start.1
  460.2 3.6 copy-start.3
  464.3 1.0 copy-start.4
  465.3 8.7 %copy-start.5 = (f32[640,1,128]{0,2,1:T(8,128)S(1)}, f32[640,1,128]{0,2,1:T(8,128)}, u32[]{:S(2)}) copy-start(f32[640,1,128]{0,2,1:T(8,128)} %get-tuple-element.183) | copy-start | bytes 983044
  466.1 9.7 %all-to-all-start.3 = ((bf16[8,80,128]{2,1,0:T(8,128)(2,1)}), bf16[8,80,128]{2,1,0:T(8,128)(2,1)S(1)}, u32[]{:S(2)}, u32[]{:S(2)}) async-start(bf16[8,80,128]{2,1,0:T(8,128)(2,1)} %bitcast.15), calls=%async_computation.3 | async-start | bytes 327680 | tf_op jit(solution)/shard_map/all_to_all | solution.py:163
  470.7 138.1 %all-reduce.12.cloned.1.call-start = ((), (), s32[]{:S(2)}) async-start(), calls=%async_computation.9 | async-start | bytes 2097152
  475.8 9.8 %all-to-all-start.4 = ((bf16[8,80,128]{2,1,0:T(8,128)(2,1)}), bf16[8,80,128]{2,1,0:T(8,128)(2,1)S(1)}, u32[]{:S(2)}, u32[]{:S(2)}) async-start(bf16[8,80,128]{2,1,0:T(8,128)(2,1)} %bitcast.17), calls=%async_computation.4 | async-start | bytes 327680 | tf_op jit(solution)/shard_map/all_to_all | solution.py:170
  498.5 6.7 %collective-permute-start = (bf16[12,1024]{1,0:T(8,128)(2,1)S(1)}, bf16[12,1024]{1,0:T(8,128)(2,1)S(1)}, u32[]{:S(2)}, u32[]{:S(2)}) collective-permute-start(bf16[12,1024]{1,0:T(8,128)(2,1)S(1)} %slice.16), channel_id=1, source_target_pairs={{0,1},{1,2},{2,3},{4,5},{5,6},{6,7},{8,9},{9,10},{10,11},{12,13},{... | collective-permute-start | bytes 73736
  499.8 5.5 collective-permute-start.1
Sparse Core Ops, SparseCore 0:
  10.7 75.5 all-gather.3
  176.1 71.4 reduce-scatter.7
  250.0 141.9 all-reduce.9
  474.2 134.5 all-reduce.11
